TPU v7x, 128 devices: a whole 4x4x4 slice. The times are simulated.
128 devices in a mesh: member: 16 (over y_lo, z, core), tile: 8 (over x, y_hi).
Axes of the slice: x: 4, y: 4 (y_hi: 2, y_lo: 2; y = y_hi * 2 + y_lo), z: 4, core: 2. Of those that a mesh axis runs over, the one named last changes fastest.
Arguments:
- ensemble: float32 [256, 4, 32, 3072], P('member', None, None, 'tile'), may hold values from -6 to 6
- kappa: float32 [4, 32, 3072], P(None, None, 'tile'), may hold values from 0.02 to 0.15
- advect: float32 [4], replicated, may hold values from 0.1 to 0.35
- observed: float32 [4, 16, 8, 768], P(None, 'member', 'tile'), may hold values from -6 to 6
- counts: int32 [4, 16, 8, 768], P(None, 'member', 'tile'), may hold values from 0 to 3
Outputs:
- analysis: float32 [256, 4, 32, 3072], P('member', None, None, 'tile')
All inputs are finite; a program needn't handle non-finite values.
Results may differ from a plain program's by a relative error of at most 0.00023.
Values sent between devices are 32-bit elements; how exact they have to be, the bound alone decides.
A program may use at most 128 MiB of HBM per device.

v0:
```python
import jax
import jax.numpy as jnp
from jax import lax
from jax.experimental import pallas as pl
from jax.experimental.pallas import tpu as pltpu
from jax.sharding import PartitionSpec as P

MESH = pl.DeviceIdType.MESH
F32 = jnp.float32
BF16 = jnp.bfloat16
LEV = 4
ROWS = 32
WIDE = 384
CELLS = 768
COLS = 48
LANES = 128
MINE = 16
K = 256
PEERS = 16
TILES = 8
ITERS = 10


def loop(count, body):
    def step(i, carry):
        body(i)
        return carry

    lax.fori_loop(0, count, step, 0)


def split3(a):
    a0 = a.astype(BF16)
    rest = a - a0.astype(F32)
    a1 = rest.astype(BF16)
    return a0, a1, (rest - a1.astype(F32)).astype(BF16)


def mm(a, b):
    return jnp.dot(a, b, preferred_element_type=F32)


def mm_t(a, b):
    return lax.dot_general(a, b, (((1,), (1,)), ((), ())), preferred_element_type=F32)


def product(a, b):
    return mm(a[0], b[0]) + (
        (mm(a[0], b[1]) + mm(a[1], b[0]))
        + (mm(a[1], b[1]) + mm(a[0], b[2]) + mm(a[2], b[0]))
    )


def swap_blocks(rows):
    turned = [pltpu.roll(r, COLS * i, 1) if i else r for i, r in enumerate(rows)]
    lane = lax.broadcasted_iota(jnp.int32, (8, LANES), 1)
    result = []
    for d in range(8):
        parts = []
        for t in range(3):
            low, high = LANES * t, LANES * (t + 1)
            first, last = low // COLS, (high - 1) // COLS
            here = [turned[(p - d) % 8][:, low:high] for p in range(first, last + 1)]
            value = here[-1]
            for p in range(last - 1, first - 1, -1):
                value = jnp.where(lane < COLS * (p + 1) - low, here[p - first], value)
            parts.append(value)
        whole = jnp.concatenate(parts, axis=1)
        result.append(pltpu.roll(whole, WIDE - COLS * d, 1) if d else whole)
    return result


def kernel(
    ens, kap, adv, obs, cnt, out,
    ensv, kapv, send_w, send_e, recv_e, recv_w, edge, kedge, u0, u1,
    snd, rcv, pert, ph, pm, pl_, qh, ql, drive, inv, root, ana, ret, outv,
    in_sem, halo_ss, halo_rs, fwd_ss, fwd_rs, own_sem, back_ss, back_rs, out_sem,
):
    me = lax.axis_index("member")
    tile = lax.axis_index("tile")
    east = lax.rem(tile + 1, TILES)
    west = lax.rem(tile + TILES - 1, TILES)

    loads = [
        pltpu.make_async_copy(ens.at[:, pl.ds(LANES * t, LANES)], ensv.at[t], in_sem.at[t]) for t in range(3)
    ] + [
        pltpu.make_async_copy(kap.at[:, pl.ds(LANES * t, LANES)], kapv.at[t], in_sem.at[3 + t]) for t in range(3)
    ]
    for load in loads:
        load.start()

    barrier = pltpu.get_barrier_semaphore()

    def greet(k):
        peer = lax.rem(me + k + 1, PEERS)
        pl.semaphore_signal(barrier, inc=1, device_id={"member": peer}, device_id_type=MESH)

    loop(PEERS - 1, greet)
    for side in (east, west):
        pl.semaphore_signal(barrier, inc=1, device_id={"tile": side}, device_id_type=MESH)

    zero_row = jnp.zeros((8, 512), F32)
    for u in (u0, u1):
        u[0] = zero_row
        u[ROWS + 1] = zero_row
    for load in loads:
        load.wait()

    lane = lax.broadcasted_iota(jnp.int32, (8, LANES), 1)

    def gather_edges(rows_of, blocks):
        def block(b, carry):
            first, last = carry
            fb = jnp.zeros((8, LANES), F32)
            lb = jnp.zeros((8, LANES), F32)
            for i in range(8):
                head, tail = rows_of(b * 8 + i)
                if i:
                    head, tail = pltpu.roll(head, 4 * i, 1), pltpu.roll(tail, 4 * i, 1)
                fb = jnp.where(lane // 4 == i, head, fb)
                lb = jnp.where(((lane + 2) % LANES) // 4 == i, tail, lb)
            fb = pltpu.roll(fb, 32 * b, 1)
            lb = pltpu.roll(lb, 32 * b, 1)
            first = jnp.where(lane // 32 == b, fb, first)
            last = jnp.where(((lane + 2) % LANES) // 32 == b, lb, last)
            return first, last

        blank = jnp.zeros((8, LANES), F32)
        return lax.fori_loop(0, blocks, block, (blank, blank))

    def edges_of(j):
        l, g = j // 2, lax.rem(j, 2)

        def rows_of(y):
            at = pl.ds(g * 1024 + l * ROWS + y, 8, stride=128)
            return ensv[0, at, :], ensv[2, at, :]

        first, last = gather_edges(rows_of, 4)
        send_w[j] = first
        send_e[j] = last

    loop(2 * LEV, edges_of)

    def kappa_rows(y):
        at = pl.ds(y, 8, stride=16)
        return kapv[0, at, :], kapv[2, at, :]

    first, last = gather_edges(kappa_rows, 2)
    send_w[2 * LEV] = first
    send_e[2 * LEV] = last

    pl.semaphore_wait(barrier, PEERS + 1)

    to_west = pltpu.make_async_remote_copy(
        send_w, recv_e, halo_ss.at[0], halo_rs.at[0], device_id={"tile": west}, device_id_type=MESH)
    to_east = pltpu.make_async_remote_copy(
        send_e, recv_w, halo_ss.at[1], halo_rs.at[1], device_id={"tile": east}, device_id_type=MESH)
    to_west.start()
    to_east.start()
    to_west.wait()
    to_east.wait()

    for j in range(2 * LEV + 1):
        edge[j] = jnp.where(lane % 4 < 2, recv_e[j], recv_w[j])

    def kappa_edges(r):
        l, q = r // 2, lax.rem(r, 2)
        row = jnp.broadcast_to(edge[2 * LEV, pl.ds(r, 1), :], (8, LANES))
        for i in range(16):
            kedge[l * ROWS + q * 16 + i] = pltpu.roll(row, LANES - 4 * i, 1) if i else row

    loop(2 * LEV, kappa_edges)

    def forward(l, k):
        peer = lax.rem(me + k + 1, PEERS)
        return pltpu.make_async_remote_copy(
            snd.at[l, peer], rcv.at[l, pl.ds(me * MINE, MINE), :], fwd_ss.at[l], fwd_rs.at[l],
            device_id={"member": peer}, device_id_type=MESH)

    def forward_own(l):
        return pltpu.make_async_copy(snd.at[l, me], rcv.at[l, pl.ds(me * MINE, MINE), :], own_sem.at[l])

    def backward(l, k):
        peer = lax.rem(me + k + 1, PEERS)
        return pltpu.make_async_remote_copy(
            ana.at[l, pl.ds(peer * MINE, MINE), :], ret.at[l, pl.ds(me * MINE, MINE), :],
            back_ss.at[l], back_rs.at[l], device_id={"member": peer}, device_id_type=MESH)

    def backward_own(l):
        at = pl.ds(me * MINE, MINE)
        return pltpu.make_async_copy(ana.at[l, at, :], ret.at[l, at, :], own_sem.at[LEV + l])

    def wait_bytes(ref, sem):
        pltpu.make_async_copy(ref, ref, sem).wait()

    def advanced(u, l, b, speed):
        rows = [u[8 * b + i] for i in range(10)]
        result = []
        for i in range(8):
            south, here, north = rows[i], rows[i + 1], rows[i + 2]
            at = l * ROWS + 8 * b + i
            kappa = jnp.concatenate(
                [jnp.broadcast_to(kapv[t, pl.ds(at, 1), :], (8, LANES)) for t in range(3)] + [kedge[at]], axis=1)
            east_cell = pltpu.roll(here, 511, 1)
            west_cell = pltpu.roll(here, 1, 1)
            laplace = east_cell + west_cell + north + south - 4.0 * here
            result.append(here + kappa * laplace + speed * (west_cell - here))
        return result

    def steps_of(l):
        speed = adv[l]

        def group(g):
            def fill(b):
                halo = pltpu.roll(edge[2 * l + g], lax.rem(LANES - 32 * b, LANES), 1)
                for i in range(8):
                    y = 8 * b + i
                    for t in range(3):
                        row = ensv[t, pl.ds(g * 1024 + l * ROWS + y, 8, stride=128), :]
                        u0[y + 1, :, LANES * t:LANES * (t + 1)] = row
                    u0[y + 1, :, WIDE:512] = pltpu.roll(halo, LANES - 4 * i, 1) if i else halo

            loop(4, fill)

            def one(b):
                for i, row in enumerate(advanced(u0, l, b, speed)):
                    u1[8 * b + i + 1] = row

            loop(4, one)

            def two(b):
                rows = [row[:, 0:WIDE] for row in advanced(u1, l, b, speed)]
                r, h = b // 2, lax.rem(b, 2)
                for c, patch in enumerate(swap_blocks(rows)):
                    snd[l, r * 8 + c, pl.ds(pl.multiple_of(g * 8, 8), 8),
                        pl.ds(pl.multiple_of(h * WIDE, LANES), WIDE)] = patch

            loop(4, two)

        loop(2, group)
        forward_own(l).start()
        loop(PEERS - 1, lambda k: forward(l, k).start())

    loop(LEV, steps_of)

    def analyse(l):
        forward_own(l).wait()
        wait_bytes(rcv.at[l, pl.ds(0, K - MINE), :], fwd_rs.at[l])

        total = jnp.zeros((8, CELLS), F32)

        def add_rows(i, total):
            block = rcv[l, pl.ds(pl.multiple_of(i * 32, 32), 32), :]
            return total + ((block[0:8] + block[8:16]) + (block[16:24] + block[24:32]))

        total = lax.fori_loop(0, 8, add_rows, total)
        mean = jnp.sum(total, axis=0, keepdims=True) * (1.0 / K)
        prec = cnt[pl.ds(l, 1), :].astype(F32) * 0.25
        weight = prec * (obs[pl.ds(l, 1), :] - mean) * (1.0 / (K - 1))

        def centre(i):
            at = pl.ds(pl.multiple_of(i * 32, 32), 32)
            block = rcv[l, at, :] - mean
            pert[at, :] = block
            p0, p1, p2 = split3(block)
            ph[at, :] = p0
            pm[at, :] = p1
            pl_[at, :] = p2
            scaled = block * prec
            q0 = scaled.astype(BF16)
            qh[at, :] = q0
            ql[at, :] = (scaled - q0.astype(F32)).astype(BF16)
            drive[at, :] = jnp.sum(block * weight, axis=1, keepdims=True)

        loop(8, centre)

        gram = mm_t(qh[...], ph[...]) + (mm_t(qh[...], pm[...]) + mm_t(ql[...], ph[...]))
        eye = jnp.where(
            lax.broadcasted_iota(jnp.int32, (K, K), 0) == lax.broadcasted_iota(jnp.int32, (K, K), 1), 1.0, 0.0)
        system = eye + gram * (1.0 / (K - 1))
        scale = jnp.sqrt(jnp.sum(jnp.sum(system * system, axis=1, keepdims=True), axis=0, keepdims=True))
        first = system * (1.0 / scale)
        factor = 1.5 * eye - 0.5 * first
        inv[...] = factor
        root[...] = product(split3(first), split3(factor))

        def newton(i):
            held, base = split3(inv[...]), split3(root[...])
            factor = split3(1.5 * eye - 0.5 * product(held, base))
            inv[...] = product(held, factor)
            root[...] = product(base, factor)

        loop(ITERS - 2, newton)
        held, base = split3(inv[...]), split3(root[...])
        factor = split3(1.5 * eye - 0.5 * product(held, base))
        half = product(held, factor) * lax.rsqrt(scale)
        inv[...] = half

        turned = jnp.sum(half * drive[...], axis=0, keepdims=True)
        drive[...] = jnp.sum(half * turned, axis=1, keepdims=True)

        def shift(i, total):
            at = pl.ds(pl.multiple_of(i * 32, 32), 32)
            block = pert[at, :] * drive[at, :]
            return total + ((block[0:8] + block[8:16]) + (block[16:24] + block[24:32]))

        total = lax.fori_loop(0, 8, shift, jnp.zeros((8, CELLS), F32))
        centre_row = mean + jnp.sum(total, axis=0, keepdims=True)
        h0, h1, h2 = split3(half)
        for c in range(3):
            at = slice(256 * c, 256 * (c + 1))
            cells = (ph[:, at], pm[:, at], pl_[:, at])
            ana[l, :, at] = centre_row[:, at] + product((h0, h1, h2), cells)

        backward_own(l).start()
        loop(PEERS - 1, lambda k: backward(l, k).start())

    loop(LEV, analyse)

    def finish(l):
        backward_own(l).wait()
        wait_bytes(ret.at[l, pl.ds(0, K - MINE), :], back_rs.at[l])

        def part(j):
            g, b = j // 4, lax.rem(j, 4)
            r, h = b // 2, lax.rem(b, 2)
            patches = [
                ret[l, pl.ds(pl.multiple_of((r * 8 + c) * MINE + g * 8, 8), 8),
                    pl.ds(pl.multiple_of(h * WIDE, LANES), WIDE)]
                for c in range(8)
            ]
            for i, row in enumerate(swap_blocks(patches)):
                for t in range(3):
                    outv[t, pl.ds(g * 1024 + l * ROWS + 8 * b + i, 8, stride=128), :] = row[:, LANES * t:LANES * (t + 1)]

        loop(8, part)

    loop(LEV, finish)
    stores = [
        pltpu.make_async_copy(outv.at[t], out.at[:, pl.ds(LANES * t, LANES)], out_sem.at[t]) for t in range(3)
    ]
    for store in stores:
        store.start()

    def drain(l):
        wait_bytes(snd.at[l, pl.ds(0, PEERS - 1)], fwd_ss.at[l])
        wait_bytes(ana.at[l, pl.ds(0, K - MINE), :], back_ss.at[l])

    loop(LEV, drain)
    for store in stores:
        store.wait()


def on_device(ensemble, kappa, advect, observed, counts):
    every = MINE * LEV * ROWS
    scratch = [
        pltpu.VMEM((3, every, LANES), F32),
        pltpu.VMEM((3, LEV * ROWS, LANES), F32),
        *[pltpu.VMEM((2 * LEV + 1, 8, LANES), F32)] * 5,
        pltpu.VMEM((LEV * ROWS, 8, LANES), F32),
        *[pltpu.VMEM((ROWS + 2, 8, 512), F32)] * 2,
        pltpu.VMEM((LEV, PEERS, MINE, CELLS), F32),
        pltpu.VMEM((LEV, K, CELLS), F32),
        pltpu.VMEM((K, CELLS), F32),
        *[pltpu.VMEM((K, CELLS), BF16)] * 5,
        pltpu.VMEM((K, 1), F32),
        *[pltpu.VMEM((K, K), F32)] * 2,
        pltpu.VMEM((LEV, K, CELLS), F32),
        pltpu.VMEM((LEV, K, CELLS), F32),
        pltpu.VMEM((3, every, LANES), F32),
        pltpu.SemaphoreType.DMA((6,)),
        *[pltpu.SemaphoreType.DMA((2,))] * 2,
        *[pltpu.SemaphoreType.DMA((LEV,))] * 2,
        pltpu.SemaphoreType.DMA((2 * LEV,)),
        *[pltpu.SemaphoreType.DMA((LEV,))] * 2,
        pltpu.SemaphoreType.DMA((3,)),
    ]
    vmem = pl.BlockSpec(memory_space=pltpu.VMEM)
    hbm = pl.BlockSpec(memory_space=pl.ANY)
    result = pl.pallas_call(
        kernel,
        out_shape=jax.ShapeDtypeStruct((every, WIDE), F32),
        in_specs=[
            hbm, hbm, pl.BlockSpec(memory_space=pltpu.SMEM), vmem, vmem],
        out_specs=pl.BlockSpec(memory_space=pl.ANY),
        scratch_shapes=scratch,
        compiler_params=pltpu.CompilerParams(
            collective_id=0, has_side_effects=True, vmem_limit_bytes=56 * 1024 * 1024),
        name="analysis",
    )(
        ensemble.reshape(every, WIDE),
        kappa.reshape(LEV * ROWS, WIDE),
        advect,
        observed.reshape(LEV, CELLS),
        counts.reshape(LEV, CELLS),
    )
    return result.reshape(MINE, LEV, ROWS, WIDE)


def solution(mesh):
    in_specs = (
        P("member", None, None, "tile"),
        P(None, None, "tile"),
        P(),
        P(None, "member", "tile", None),
        P(None, "member", "tile", None),
    )
    return jax.shard_map(
        on_device, mesh=mesh, in_specs=in_specs, out_specs=P("member", None, None, "tile"), check_vma=False
    )
```

profile of v0, /device:TPU:1, one launch (start us, length us, event | category | flops | bytes accessed | tf_op | source)
XLA Modules:
  0.0 110.5 jit_solution(15163880640784198705)
XLA Ops:
  0.0 1.3 %copy.11 = f32[4,1,1,768]{3,0,1,2:T(4,128)} copy(f32[4,1,1,768]{3,2,1,0:T(1,128)} %param.8) | data formatting | bytes 24576
  1.3 1.3 %copy.10 = s32[4,1,1,768]{3,0,1,2:T(4,128)} copy(s32[4,1,1,768]{3,2,1,0:T(1,128)} %param.9) | data formatting | bytes 24576
  2.6 104.1 %analysis.1 = f32[2048,384]{1,0:T(8,128)} custom-call(f32[2048,384]{1,0:T(8,128)} %bitcast.10, f32[128,384]{1,0:T(8,128)} %bitcast.11, f32[4]{0:T(128)} %adv.1, f32[4,768]{1,0:T(4,128)} %bitcast.12, s32[4,768]{1,0:T(4,128)} %bitcast.13), custom_call_target="tpu_custom_call" | custom-call | tf_op jit(solution)/shard_map/analysis/pallas_call | solution.py:380
  106.7 3.8 %copy.13 = f32[16,4,32,384]{3,2,1,0:T(8,128)} copy(f32[16,4,32,384]{3,2,1,0:T(8,128)} %bitcast.9) | data formatting | bytes 6291456
where the time goes:
time: 111 us
  Pallas kernels  104 us (94%)
  local copies, waits for them, and re-layouts  6.45 us (6%)
    pallas_call x1, Pallas kernels, on_device(): pl.pallas_call(kernel, out_shape=jax.ShapeDtypeStruct((every, WIDE), F32)...  104 us
    unnamed x3, local copies, waits for them, and re-layouts  6.45 us

commit v1 on v0

v1 whole, which is shorter than its diff:
```python
import jax
import jax.numpy as jnp
from jax import lax
from jax.experimental import pallas as pl
from jax.experimental.pallas import tpu as pltpu
from jax.sharding import PartitionSpec as P

MESH = pl.DeviceIdType.MESH
F32 = jnp.float32
BF16 = jnp.bfloat16
LEV = 4
ROWS = 32
PAD = ROWS + 2
WIDE = 384
CELLS = 768
COLS = 48
LANES = 128
MINE = 16
FIELDS = 24
CHUNK = 64
K = 256
PEERS = 16
TILES = 8
ITERS = 10


def loop(count, body):
    def step(i, carry):
        body(i)
        return carry

    lax.fori_loop(0, count, step, 0)


def split3(a):
    a0 = a.astype(BF16)
    rest = a - a0.astype(F32)
    a1 = rest.astype(BF16)
    return a0, a1, (rest - a1.astype(F32)).astype(BF16)


def mm(a, b):
    return jnp.dot(a, b, preferred_element_type=F32)


def mm_t(a, b):
    return lax.dot_general(a, b, (((1,), (1,)), ((), ())), preferred_element_type=F32)


def product(a, b):
    return mm(a[0], b[0]) + (
        (mm(a[0], b[1]) + mm(a[1], b[0]))
        + (mm(a[1], b[1]) + mm(a[0], b[2]) + mm(a[2], b[0]))
    )


def sheared(arrays):
    lane = lax.broadcasted_iota(jnp.int32, (MINE, LANES), 1)
    result = []
    for d in range(8):
        parts = []
        for t in range(3):
            low, high = LANES * t, LANES * (t + 1)
            first, last = low // COLS, (high - 1) // COLS
            here = [arrays[(p - d) % 8][:, low:high] for p in range(first, last + 1)]
            value = here[-1]
            for p in range(last - 1, first - 1, -1):
                value = jnp.where(lane < COLS * (p + 1) - low, here[p - first], value)
            parts.append(value)
        result.append(jnp.concatenate(parts, axis=1))
    return result


def turned(array, shift):
    shift %= array.shape[1]
    return pltpu.roll(array, shift, 1) if shift else array


def moved(here, east, west, north, south, kappa, speed):
    return here + kappa * (east + west + north + south - 4.0 * here) + speed * (west - here)


def kernel(
    ens, kap, adv, obs, cnt, out,
    ensv, send_w, send_e, recv_e, recv_w, mend_w, mend_e, u1,
    snd, rcv, pert, ph, pm, pl_, qh, ql, drive, inv, root, ana, ret, outv,
    in_sem, halo_ss, halo_rs, fwd_ss, fwd_rs, own_sem, back_ss, back_rs, out_sem,
):
    me = lax.axis_index("member")
    tile = lax.axis_index("tile")
    east = lax.rem(tile + 1, TILES)
    west = lax.rem(tile + TILES - 1, TILES)
    inner = pl.ds(1, ROWS)

    def load_levels(part, base, count):
        levels = pl.ds(base, count)

        def member(m):
            pltpu.make_async_copy(
                ens.at[m, levels], ensv.at[levels, inner, m, :], in_sem.at[part]).start()

        def copy_kappa(m):
            pltpu.make_async_copy(
                kap.at[levels], ensv.at[levels, inner, MINE + m, :], in_sem.at[part]).start()

        loop(MINE, member)
        loop(FIELDS - MINE, copy_kappa)

    load_levels(0, 0, 1)
    load_levels(1, 1, LEV - 1)

    barrier = pltpu.get_barrier_semaphore()

    def greet(k):
        peer = lax.rem(me + k + 1, PEERS)
        pl.semaphore_signal(barrier, inc=1, device_id={"member": peer}, device_id_type=MESH)

    loop(PEERS - 1, greet)
    for side in (east, west):
        pl.semaphore_signal(barrier, inc=1, device_id={"tile": side}, device_id_type=MESH)

    def clear(l):
        for y in (0, ROWS + 1):
            ensv[l, y] = jnp.zeros((FIELDS, WIDE), F32)
            u1[l, y] = jnp.zeros((MINE, WIDE), F32)

    loop(LEV, clear)

    def wait_bytes(ref, sem):
        pltpu.make_async_copy(ref, ref, sem).wait()

    wait_bytes(ensv.at[pl.ds(0, 1), inner], in_sem.at[0])

    def step_one(l, b):
        rows = [ensv[l, 8 * b + i, 0:MINE] for i in range(10)]
        speed = adv[l]
        for i in range(8):
            south, here, north = rows[i:i + 3]
            kappa = ensv[l, 8 * b + i + 1, MINE:FIELDS]
            kappa = jnp.concatenate([kappa, kappa], axis=0)
            u1[l, 8 * b + i + 1] = moved(here, turned(here, -1), turned(here, 1), north, south, kappa, speed)

    def step_two(l, b):
        rows = [u1[l, 8 * b + i] for i in range(10)]
        speed = adv[l]
        done = []
        for i in range(8):
            south, here, north = rows[i:i + 3]
            kappa = ensv[l, 8 * b + i + 1, MINE:FIELDS]
            kappa = jnp.concatenate([kappa, kappa], axis=0)
            row = moved(here, turned(here, -1), turned(here, 1), north, south, kappa, speed)
            done.append(turned(row, COLS * i))
        r, h = b // 2, lax.rem(b, 2)
        for c, patch in enumerate(sheared(done)):
            snd[l, r * 8 + c, :, pl.ds(pl.multiple_of(h * WIDE, LANES), WIDE)] = patch

    loop(4, lambda b: step_one(0, b))
    wait_bytes(ensv.at[pl.ds(1, LEV - 1), inner], in_sem.at[1])

    lane = lax.broadcasted_iota(jnp.int32, (FIELDS, LANES), 1)

    def edges_of(l):
        first = jnp.zeros((FIELDS, LANES), F32)
        last = jnp.zeros((FIELDS, LANES), F32)
        for y in range(ROWS):
            ends = jnp.where(lane < 64, ensv[l, y + 1, :, 0:LANES], ensv[l, y + 1, :, 2 * LANES:3 * LANES])
            ends = turned(ends, 4 * y)
            first = jnp.where(lane // 4 == y, ends, first)
            last = jnp.where(lane // 4 == (y - 1) % ROWS, ends, last)
        send_w[l] = first
        send_e[l] = turned(last, 4)

    loop(LEV, edges_of)
    pl.semaphore_wait(barrier, PEERS + 1)

    to_west = pltpu.make_async_remote_copy(
        send_w, recv_e, halo_ss.at[0], halo_rs.at[0], device_id={"tile": west}, device_id_type=MESH)
    to_east = pltpu.make_async_remote_copy(
        send_e, recv_w, halo_ss.at[1], halo_rs.at[1], device_id={"tile": east}, device_id_type=MESH)
    to_west.start()
    to_east.start()

    def forward(l, peer):
        return pltpu.make_async_remote_copy(
            snd.at[l, peer], rcv.at[l, pl.ds(me * MINE, MINE), :], fwd_ss.at[l], fwd_rs.at[l],
            device_id={"member": peer}, device_id_type=MESH)

    def forward_own(l):
        return pltpu.make_async_copy(snd.at[l, me], rcv.at[l, pl.ds(me * MINE, MINE), :], own_sem.at[l])

    def backward(l, k):
        peer = lax.rem(me + k + 1, PEERS)
        return pltpu.make_async_remote_copy(
            ana.at[l, pl.ds(peer * MINE, MINE), :], ret.at[l, pl.ds(me * MINE, MINE), :],
            back_ss.at[l], back_rs.at[l], device_id={"member": peer}, device_id_type=MESH)

    def backward_own(l):
        at = pl.ds(me * MINE, MINE)
        return pltpu.make_async_copy(ana.at[l, at, :], ret.at[l, at, :], own_sem.at[LEV + l])

    def send(l, wanted):
        def one(k):
            peer = lax.rem(me + k, PEERS)
            column = lax.rem(peer, 8)
            outer = jnp.logical_or(column == 0, column == 7)

            @pl.when(outer if wanted else jnp.logical_not(outer))
            def _():
                @pl.when(k == 0)
                def _():
                    forward_own(l).start()

                @pl.when(k > 0)
                def _():
                    forward(l, peer).start()

        loop(PEERS, one)

    def compact(a, b, ka, kb, speed, want_a, want_b):
        place = lax.broadcasted_iota(jnp.int32, a.shape, 1)
        slot = place % 4

        def sides(x):
            south = jnp.where(place < 4, 0.0, pltpu.roll(x, 4, 1))
            north = jnp.where(place >= LANES - 4, 0.0, pltpu.roll(x, LANES - 4, 1))
            return north, south

        new_a = new_b = None
        if want_a:
            after = jnp.where(slot == 3, pltpu.roll(b, 3, 1), pltpu.roll(a, LANES - 1, 1))
            new_a = moved(a, after, pltpu.roll(a, 1, 1), *sides(a), ka, speed)
        if want_b:
            before = jnp.where(slot == 0, pltpu.roll(a, LANES - 3, 1), pltpu.roll(b, 1, 1))
            new_b = moved(b, pltpu.roll(b, LANES - 1, 1), before, *sides(b), kb, speed)
        return new_a, new_b

    def mend_edges(l):
        speed = adv[l]

        def parts(ref):
            kappa = ref[l, MINE:FIELDS]
            return ref[l, 0:MINE], jnp.concatenate([kappa, kappa], axis=0)

        (a, ka), (b, kb) = parts(recv_w), parts(send_w)
        a, b = compact(a, b, ka, kb, speed, True, True)
        mend_w[l] = compact(a, b, ka, kb, speed, False, True)[1]
        (a, ka), (b, kb) = parts(send_e), parts(recv_e)
        a, b = compact(a, b, ka, kb, speed, True, True)
        mend_e[l] = compact(a, b, ka, kb, speed, True, False)[0]

    def insert_edges(l):
        place = lax.broadcasted_iota(jnp.int32, (MINE, LANES), 1)
        for mend, c, cell in ((mend_w, 0, 0), (mend_e, 7, COLS - 2)):
            values = mend[l]
            for b in range(4):
                r, h = divmod(b, 2)
                tiles = [snd[l, r * 8 + c, :, WIDE * h + LANES * t:WIDE * h + LANES * (t + 1)] for t in range(3)]
                for i in range(8):
                    to = COLS * ((c + i) % 8) + cell
                    t, to = divmod(to, LANES)
                    source = 4 * (8 * b + i) + (2 if cell else 0)
                    value = turned(values, to - source)
                    tiles[t] = jnp.where(jnp.logical_or(place == to, place == to + 1), value, tiles[t])
                for t in range(3):
                    snd[l, r * 8 + c, :, WIDE * h + LANES * t:WIDE * h + LANES * (t + 1)] = tiles[t]

    def two_steps(l, follow):
        def body(b):
            step_two(l, b)
            if follow:
                step_one(l + 1, b)

        loop(4, body)

    def finish_edges(l):
        insert_edges(l)
        send(l, True)

    two_steps(0, True)
    send(0, False)
    two_steps(1, True)
    to_west.wait()
    to_east.wait()
    loop(LEV, mend_edges)
    finish_edges(0)
    send(1, False)
    finish_edges(1)

    two_steps(2, True)
    send(2, False)
    finish_edges(2)
    two_steps(3, False)
    send(3, False)
    finish_edges(3)

    order = COLS * lax.rem(me, 8)

    def ordered(row):
        row = jnp.broadcast_to(row, (8, CELLS))
        return jnp.concatenate(
            [pltpu.roll(row[:, WIDE * h:WIDE * (h + 1)], order, 1) for h in range(2)], axis=1)[0:1]

    def analyse(l):
        forward_own(l).wait()
        wait_bytes(rcv.at[l, pl.ds(0, K - MINE), :], fwd_rs.at[l])
        total = jnp.zeros((8, CELLS), F32)

        def add_rows(i, total):
            block = rcv[l, pl.ds(pl.multiple_of(i * CHUNK, CHUNK), CHUNK), :]
            return total + jnp.sum(block.reshape(CHUNK // 8, 8, CELLS), axis=0)

        total = lax.fori_loop(0, K // CHUNK, add_rows, total)
        mean = jnp.sum(total, axis=0, keepdims=True) * (1.0 / K)
        prec = ordered(cnt[l].astype(F32)) * 0.25
        weight = prec * (ordered(obs[l]) - mean) * (1.0 / (K - 1))

        def centre(i):
            at = pl.ds(pl.multiple_of(i * CHUNK, CHUNK), CHUNK)
            block = rcv[l, at, :] - mean
            pert[at, :] = block
            p0, p1, p2 = split3(block)
            ph[at, :] = p0
            pm[at, :] = p1
            pl_[at, :] = p2
            scaled = block * prec
            q0 = scaled.astype(BF16)
            qh[at, :] = q0
            ql[at, :] = (scaled - q0.astype(F32)).astype(BF16)
            drive[at, :] = jnp.sum(block * weight, axis=1, keepdims=True)

        loop(K // CHUNK, centre)

        gram = mm_t(qh[...], ph[...]) + (mm_t(qh[...], pm[...]) + mm_t(ql[...], ph[...]))
        eye = jnp.where(
            lax.broadcasted_iota(jnp.int32, (K, K), 0) == lax.broadcasted_iota(jnp.int32, (K, K), 1), 1.0, 0.0)
        system = eye + gram * (1.0 / (K - 1))
        scale = jnp.sqrt(jnp.sum(jnp.sum(system * system, axis=1, keepdims=True), axis=0, keepdims=True))
        first = system * (1.0 / scale)
        factor = 1.5 * eye - 0.5 * first
        inv[...] = factor
        root[...] = product(split3(first), split3(factor))

        def newton(i):
            held, base = split3(inv[...]), split3(root[...])
            factor = split3(1.5 * eye - 0.5 * product(held, base))
            inv[...] = product(held, factor)
            root[...] = product(base, factor)

        loop(ITERS - 2, newton)
        held, base = split3(inv[...]), split3(root[...])
        factor = split3(1.5 * eye - 0.5 * product(held, base))
        half = product(held, factor) * lax.rsqrt(scale)
        inv[...] = half

        turned = jnp.sum(half * drive[...], axis=0, keepdims=True)
        drive[...] = jnp.sum(half * turned, axis=1, keepdims=True)

        def shift(i, total):
            at = pl.ds(pl.multiple_of(i * CHUNK, CHUNK), CHUNK)
            block = pert[at, :] * drive[at, :]
            return total + jnp.sum(block.reshape(CHUNK // 8, 8, CELLS), axis=0)

        total = lax.fori_loop(0, K // CHUNK, shift, jnp.zeros((8, CELLS), F32))
        centre_row = mean + jnp.sum(total, axis=0, keepdims=True)
        h0, h1, h2 = split3(half)
        for c in range(3):
            at = slice(256 * c, 256 * (c + 1))
            cells = (ph[:, at], pm[:, at], pl_[:, at])
            ana[l, :, at] = centre_row[:, at] + product((h0, h1, h2), cells)

        backward_own(l).start()
        loop(PEERS - 1, lambda k: backward(l, k).start())

    loop(LEV, analyse)

    def finish(l):
        backward_own(l).wait()
        wait_bytes(ret.at[l, pl.ds(0, K - MINE), :], back_rs.at[l])

        def part(b):
            r, h = b // 2, lax.rem(b, 2)
            patches = [
                ret[l, pl.ds(pl.multiple_of((r * 8 + c) * MINE, MINE), MINE),
                    pl.ds(pl.multiple_of(h * WIDE, LANES), WIDE)]
                for c in range(8)
            ]
            for i, row in enumerate(sheared(patches)):
                outv[l, 8 * b + i] = turned(row, -COLS * i)

        loop(4, part)

        def member(m):
            pltpu.make_async_copy(outv.at[l, :, m, :], out.at[m, l], out_sem.at[l]).start()

        loop(MINE, member)

    loop(LEV, finish)

    def drain(l):
        wait_bytes(snd.at[l, pl.ds(0, PEERS - 1)], fwd_ss.at[l])
        wait_bytes(ana.at[l, pl.ds(0, K - MINE), :], back_ss.at[l])
        wait_bytes(outv.at[l], out_sem.at[l])

    loop(LEV, drain)


def on_device(ensemble, kappa, advect, observed, counts):
    scratch = [
        pltpu.VMEM((LEV, PAD, FIELDS, WIDE), F32),
        *[pltpu.VMEM((LEV, FIELDS, LANES), F32)] * 4,
        *[pltpu.VMEM((LEV, MINE, LANES), F32)] * 2,
        pltpu.VMEM((LEV, PAD, MINE, WIDE), F32),
        pltpu.VMEM((LEV, PEERS, MINE, CELLS), F32),
        pltpu.VMEM((LEV, K, CELLS), F32),
        pltpu.VMEM((K, CELLS), F32),
        *[pltpu.VMEM((K, CELLS), BF16)] * 5,
        pltpu.VMEM((K, 1), F32),
        *[pltpu.VMEM((K, K), F32)] * 2,
        pltpu.VMEM((LEV, K, CELLS), F32),
        pltpu.VMEM((LEV, K, CELLS), F32),
        pltpu.VMEM((LEV, ROWS, MINE, WIDE), F32),
        pltpu.SemaphoreType.DMA((2,)),
        *[pltpu.SemaphoreType.DMA((2,))] * 2,
        *[pltpu.SemaphoreType.DMA((LEV,))] * 2,
        pltpu.SemaphoreType.DMA((2 * LEV,)),
        *[pltpu.SemaphoreType.DMA((LEV,))] * 2,
        pltpu.SemaphoreType.DMA((LEV,)),
    ]
    vmem = pl.BlockSpec(memory_space=pltpu.VMEM)
    hbm = pl.BlockSpec(memory_space=pl.ANY)
    return pl.pallas_call(
        kernel,
        out_shape=jax.ShapeDtypeStruct((MINE, LEV, ROWS, WIDE), F32),
        in_specs=[hbm, hbm, pl.BlockSpec(memory_space=pltpu.SMEM), vmem, vmem],
        out_specs=hbm,
        scratch_shapes=scratch,
        compiler_params=pltpu.CompilerParams(
            collective_id=0, has_side_effects=True, vmem_limit_bytes=56 * 1024 * 1024),
        name="analysis",
    )(ensemble, kappa, advect, observed.reshape(LEV, 1, CELLS), counts.reshape(LEV, 1, CELLS))


def solution(mesh):
    in_specs = (
        P("member", None, None, "tile"),
        P(None, None, "tile"),
        P(),
        P(None, "member", "tile", None),
        P(None, "member", "tile", None),
    )
    return jax.shard_map(
        on_device, mesh=mesh, in_specs=in_specs, out_specs=P("member", None, None, "tile"), check_vma=False
    )
```

time: 111 us -> 91.2 us (0.82)
  Pallas kernels: 104 us -> 86.2 us
  local copies, waits for them, and re-layouts: 6.45 us -> 3.83 us
    pallas_call x1, Pallas kernels: 104 us -> 86.2 us  [on_device(): pl.pallas_call(kernel, out_shape=jax.ShapeDtypeStruct((MINE, LEV, ROWS, W...]
    unnamed x3 -> x1, local copies, waits for them, and re-layouts: 6.45 us -> 3.83 us
where the time goes in v1:
time: 91.2 us; the launch traced here: 90.1 us
  Pallas kernels  86.2 us (95%)
  local copies, waits for them, and re-layouts  3.83 us (4%)
    pallas_call x1, Pallas kernels, on_device(): pl.pallas_call(kernel, out_shape=jax.ShapeDtypeStruct((MINE, LEV, ROWS, W...  86.2 us
    unnamed x1, local copies, waits for them, and re-layouts  3.83 us

profile of v1, /device:TPU:1, one launch (start us, length us, event | category | flops | bytes accessed | tf_op | source)
XLA Modules:
  0.0 90.1 jit_solution(6939107647301580465)
XLA Ops:
  0.0 86.2 %analysis.1 = f32[16,4,32,384]{3,2,1,0:T(8,128)} custom-call(f32[16,4,32,384]{3,2,1,0:T(8,128)} %ens.1, f32[4,32,384]{2,1,0:T(8,128)} %kap.1, f32[4]{0:T(128)} %adv.1, f32[4,1,768]{2,1,0:T(1,128)} %bitcast.2, s32[4,1,768]{2,1,0:T(1,128)} %bitcast.3), custom_call_target="tpu_custom_call" | custom-call | tf_op jit(solution)/shard_map/analysis/pallas_call | solution.py:431
  86.2 3.8 %copy.7 = f32[16,4,32,384]{3,2,1,0:T(8,128)} copy(f32[16,4,32,384]{3,2,1,0:T(8,128)} %analysis.1) | data formatting | bytes 6291456

commit v2 on v1

--- a/solution.py
+++ b/solution.py
@@ -81,7 +81,7 @@
 
 
 def kernel(
-    ens, kap, adv, obs, cnt, out,
+    ens, kap, adv, obs, cnt, field,
     ensv, send_w, send_e, recv_e, recv_w, mend_w, mend_e, u1,
     snd, rcv, pert, ph, pm, pl_, qh, ql, drive, inv, root, ana, ret, outv,
     in_sem, halo_ss, halo_rs, fwd_ss, fwd_rs, own_sem, back_ss, back_rs, out_sem,
@@ -385,23 +385,26 @@
                 for c in range(8)
             ]
             for i, row in enumerate(sheared(patches)):
-                outv[l, 8 * b + i] = turned(row, -COLS * i)
+                field[l, 8 * b + i] = turned(row, -COLS * i)
 
         loop(4, part)
 
-        def member(m):
-            pltpu.make_async_copy(outv.at[l, :, m, :], out.at[m, l], out_sem.at[l]).start()
-
-        loop(MINE, member)
 
     loop(LEV, finish)
 
     def drain(l):
         wait_bytes(snd.at[l, pl.ds(0, PEERS - 1)], fwd_ss.at[l])
         wait_bytes(ana.at[l, pl.ds(0, K - MINE), :], back_ss.at[l])
-        wait_bytes(outv.at[l], out_sem.at[l])
 
     loop(LEV, drain)
+
+
+def members_first(field, out, sem):
+    def copy(m):
+        return pltpu.make_async_copy(field.at[:, :, m, :], out.at[m], sem)
+
+    loop(MINE, lambda m: copy(m).start())
+    pltpu.make_async_copy(field, field, sem).wait()
 
 
 def on_device(ensemble, kappa, advect, observed, counts):
@@ -427,17 +430,27 @@
         pltpu.SemaphoreType.DMA((LEV,)),
     ]
     vmem = pl.BlockSpec(memory_space=pltpu.VMEM)
-    hbm = pl.BlockSpec(memory_space=pl.ANY)
-    return pl.pallas_call(
+    whole = pl.BlockSpec(memory_space=pl.ANY)
+    smem = pl.BlockSpec(memory_space=pltpu.SMEM)
+    members_last = pl.pallas_call(
         kernel,
-        out_shape=jax.ShapeDtypeStruct((MINE, LEV, ROWS, WIDE), F32),
-        in_specs=[hbm, hbm, pl.BlockSpec(memory_space=pltpu.SMEM), vmem, vmem],
-        out_specs=hbm,
+        out_shape=pltpu.VMEM((LEV, ROWS, MINE, WIDE), F32),
+        in_specs=[whole, whole, smem, vmem, vmem],
+        out_specs=vmem,
         scratch_shapes=scratch,
         compiler_params=pltpu.CompilerParams(
             collective_id=0, has_side_effects=True, vmem_limit_bytes=56 * 1024 * 1024),
         name="analysis",
     )(ensemble, kappa, advect, observed.reshape(LEV, 1, CELLS), counts.reshape(LEV, 1, CELLS))
+    return pl.pallas_call(
+        members_first,
+        out_shape=jax.ShapeDtypeStruct((MINE, LEV, ROWS, WIDE), F32),
+        in_specs=[whole],
+        out_specs=whole,
+        scratch_shapes=[pltpu.SemaphoreType.DMA],
+        compiler_params=pltpu.CompilerParams(vmem_limit_bytes=1024 * 1024),
+        name="members_first",
+    )(members_last)
 
 
 def solution(mesh):

time: 91.2 us -> 87.9 us (0.964)
  local copies, waits for them, and re-layouts: 3.83 us -> 0 us
    unnamed x1 -> x0, local copies, waits for them, and re-layouts: 3.83 us -> none
    pallas_call x1 -> x2, Pallas kernels: 86.2 us -> 87 us  [the longest x1 85.4 us: on_device(): pl.pallas_call(kernel, out_shape=pltpu.VMEM((LEV, ROWS, MINE, WIDE), F32)...]
where the time goes in v2:
time: 87.9 us; the launch traced here: 87 us
  Pallas kernels  87 us (99%)
    pallas_call x1, Pallas kernels, on_device(): pl.pallas_call(kernel, out_shape=pltpu.VMEM((LEV, ROWS, MINE, WIDE), F32)...  85.4 us

profile of v2, /device:TPU:1, one launch (start us, length us, event | category | flops | bytes accessed | tf_op | source)
XLA Modules:
  0.0 87.0 jit_solution(5729538426181245954)
XLA Ops:
  0.0 85.4 %analysis.1.field = f32[4,32,16,384]{3,2,1,0:T(8,128)S(1)} custom-call(f32[16,4,32,384]{3,2,1,0:T(8,128)} %ens.1, f32[4,32,384]{2,1,0:T(8,128)} %kap.1, f32[4]{0:T(128)} %adv.1, f32[4,1,768]{2,1,0:T(1,128)} %bitcast.2, s32[4,1,768]{2,1,0:T(1,128)} %bitcast.3), custom_call_target="tpu_custom_call" | custom-call | tf_op jit(solution)/shard_map/analysis/pallas_call | solution.py:435
  85.4 1.7 %members_first.1 = f32[16,4,32,384]{3,2,1,0:T(8,128)} custom-call(f32[4,32,16,384]{3,2,1,0:T(8,128)S(1)} %analysis.1.field), custom_call_target="tpu_custom_call" | custom-call | tf_op jit(solution)/shard_map/members_first/pallas_call | solution.py:445

commit v3 on v2

--- a/solution.py
+++ b/solution.py
@@ -17,7 +17,7 @@
 LANES = 128
 MINE = 16
 FIELDS = 24
-CHUNK = 64
+CHUNK = 256
 K = 256
 PEERS = 16
 TILES = 8
@@ -82,8 +82,8 @@
 
 def kernel(
     ens, kap, adv, obs, cnt, field,
-    ensv, send_w, send_e, recv_e, recv_w, mend_w, mend_e, u1,
-    snd, rcv, pert, ph, pm, pl_, qh, ql, drive, inv, root, ana, ret, outv,
+    ensv, head, tail, send_w, send_e, recv_e, recv_w, mend_w, mend_e, u1,
+    snd, rcv, ph, pm, pl_, qh, ql, drive, inv, root, ana, ret, outv,
     in_sem, halo_ss, halo_rs, fwd_ss, fwd_rs, own_sem, back_ss, back_rs, out_sem,
 ):
     me = lax.axis_index("member")
@@ -155,6 +155,7 @@
             snd[l, r * 8 + c, :, pl.ds(pl.multiple_of(h * WIDE, LANES), WIDE)] = patch
 
     loop(4, lambda b: step_one(0, b))
+    loop(4, lambda b: step_two(0, b))
     wait_bytes(ensv.at[pl.ds(1, LEV - 1), inner], in_sem.at[1])
 
     lane = lax.broadcasted_iota(jnp.int32, (FIELDS, LANES), 1)
@@ -167,10 +168,13 @@
             ends = turned(ends, 4 * y)
             first = jnp.where(lane // 4 == y, ends, first)
             last = jnp.where(lane // 4 == (y - 1) % ROWS, ends, last)
-        send_w[l] = first
-        send_e[l] = turned(last, 4)
+        head[l] = first
+        tail[l] = turned(last, 4)
 
     loop(LEV, edges_of)
+    for j in range(LEV // 2):
+        send_w[j] = jnp.where(lane % 4 < 2, head[2 * j], turned(head[2 * j + 1], 2))
+        send_e[j] = jnp.where(lane % 4 < 2, turned(tail[2 * j + 1], -2), tail[2 * j])
     pl.semaphore_wait(barrier, PEERS + 1)
 
     to_west = pltpu.make_async_remote_copy(
@@ -237,14 +241,17 @@
     def mend_edges(l):
         speed = adv[l]
 
-        def parts(ref):
-            kappa = ref[l, MINE:FIELDS]
-            return ref[l, 0:MINE], jnp.concatenate([kappa, kappa], axis=0)
-
-        (a, ka), (b, kb) = parts(recv_w), parts(send_w)
+        def parts(both):
+            kappa = both[MINE:FIELDS]
+            return both[0:MINE], jnp.concatenate([kappa, kappa], axis=0)
+
+        from_west, from_east = recv_w[l // 2], recv_e[l // 2]
+        if l % 2:
+            from_west, from_east = turned(from_west, 2), turned(from_east, -2)
+        (a, ka), (b, kb) = parts(from_west), parts(head[l])
         a, b = compact(a, b, ka, kb, speed, True, True)
         mend_w[l] = compact(a, b, ka, kb, speed, False, True)[1]
-        (a, ka), (b, kb) = parts(send_e), parts(recv_e)
+        (a, ka), (b, kb) = parts(tail[l]), parts(from_east)
         a, b = compact(a, b, ka, kb, speed, True, True)
         mend_e[l] = compact(a, b, ka, kb, speed, True, False)[0]
 
@@ -273,15 +280,15 @@
         loop(4, body)
 
     def finish_edges(l):
+        mend_edges(l)
         insert_edges(l)
         send(l, True)
 
-    two_steps(0, True)
     send(0, False)
+    loop(4, lambda b: step_one(1, b))
     two_steps(1, True)
     to_west.wait()
     to_east.wait()
-    loop(LEV, mend_edges)
     finish_edges(0)
     send(1, False)
     finish_edges(1)
@@ -317,7 +324,6 @@
         def centre(i):
             at = pl.ds(pl.multiple_of(i * CHUNK, CHUNK), CHUNK)
             block = rcv[l, at, :] - mean
-            pert[at, :] = block
             p0, p1, p2 = split3(block)
             ph[at, :] = p0
             pm[at, :] = p1
@@ -350,23 +356,14 @@
         held, base = split3(inv[...]), split3(root[...])
         factor = split3(1.5 * eye - 0.5 * product(held, base))
         half = product(held, factor) * lax.rsqrt(scale)
-        inv[...] = half
-
-        turned = jnp.sum(half * drive[...], axis=0, keepdims=True)
-        drive[...] = jnp.sum(half * turned, axis=1, keepdims=True)
-
-        def shift(i, total):
-            at = pl.ds(pl.multiple_of(i * CHUNK, CHUNK), CHUNK)
-            block = pert[at, :] * drive[at, :]
-            return total + jnp.sum(block.reshape(CHUNK // 8, 8, CELLS), axis=0)
-
-        total = lax.fori_loop(0, K // CHUNK, shift, jnp.zeros((8, CELLS), F32))
-        centre_row = mean + jnp.sum(total, axis=0, keepdims=True)
-        h0, h1, h2 = split3(half)
+
+        once = jnp.sum(half * drive[...], axis=0, keepdims=True)
+        twice = jnp.sum(half * once, axis=1, keepdims=True)
+        w0, w1, w2 = split3(half + jnp.sum(eye * twice, axis=0, keepdims=True))
         for c in range(3):
             at = slice(256 * c, 256 * (c + 1))
             cells = (ph[:, at], pm[:, at], pl_[:, at])
-            ana[l, :, at] = centre_row[:, at] + product((h0, h1, h2), cells)
+            ana[l, :, at] = mean[:, at] + product((w0, w1, w2), cells)
 
         backward_own(l).start()
         loop(PEERS - 1, lambda k: backward(l, k).start())
@@ -410,12 +407,12 @@
 def on_device(ensemble, kappa, advect, observed, counts):
     scratch = [
         pltpu.VMEM((LEV, PAD, FIELDS, WIDE), F32),
-        *[pltpu.VMEM((LEV, FIELDS, LANES), F32)] * 4,
+        *[pltpu.VMEM((LEV, FIELDS, LANES), F32)] * 2,
+        *[pltpu.VMEM((LEV // 2, FIELDS, LANES), F32)] * 4,
         *[pltpu.VMEM((LEV, MINE, LANES), F32)] * 2,
         pltpu.VMEM((LEV, PAD, MINE, WIDE), F32),
         pltpu.VMEM((LEV, PEERS, MINE, CELLS), F32),
         pltpu.VMEM((LEV, K, CELLS), F32),
-        pltpu.VMEM((K, CELLS), F32),
         *[pltpu.VMEM((K, CELLS), BF16)] * 5,
         pltpu.VMEM((K, 1), F32),
         *[pltpu.VMEM((K, K), F32)] * 2,

time: 87.9 us -> 84.7 us (0.964)
  Pallas kernels: 87 us -> 84.5 us
    pallas_call x1, Pallas kernels: 85.4 us -> 82.9 us  [on_device(): pl.pallas_call(kernel, out_shape=pltpu.VMEM((LEV, ROWS, MINE, WIDE), F32)...]
where the time goes in v3:
time: 84.7 us; the launch traced here: 84.5 us
  Pallas kernels  84.5 us (100%)
    pallas_call x1, Pallas kernels, on_device(): pl.pallas_call(kernel, out_shape=pltpu.VMEM((LEV, ROWS, MINE, WIDE), F32)...  82.9 us

profile of v3, /device:TPU:1, one launch (start us, length us, event | category | flops | bytes accessed | tf_op | source)
XLA Modules:
  0.0 84.5 jit_solution(12295159056263495431)
XLA Ops:
  0.0 82.9 %analysis.1.field = f32[4,32,16,384]{3,2,1,0:T(8,128)S(1)} custom-call(f32[16,4,32,384]{3,2,1,0:T(8,128)} %ens.1, f32[4,32,384]{2,1,0:T(8,128)} %kap.1, f32[4]{0:T(128)} %adv.1, f32[4,1,768]{2,1,0:T(1,128)} %bitcast.2, s32[4,1,768]{2,1,0:T(1,128)} %bitcast.3), custom_call_target="tpu_custom_call" | custom-call | tf_op jit(solution)/shard_map/analysis/pallas_call | solution.py:432
  82.9 1.7 %members_first.1 = f32[16,4,32,384]{3,2,1,0:T(8,128)} custom-call(f32[4,32,16,384]{3,2,1,0:T(8,128)S(1)} %analysis.1.field), custom_call_target="tpu_custom_call" | custom-call | tf_op jit(solution)/shard_map/members_first/pallas_call | solution.py:442

commit v4 on v3

--- a/solution.py
+++ b/solution.py
@@ -82,7 +82,7 @@
 
 def kernel(
     ens, kap, adv, obs, cnt, field,
-    ensv, head, tail, send_w, send_e, recv_e, recv_w, mend_w, mend_e, u1,
+    ensv, kapv, head, tail, send_w, send_e, recv_e, recv_w, mend_w, mend_e, u1,
     snd, rcv, ph, pm, pl_, qh, ql, drive, inv, root, ana, ret, outv,
     in_sem, halo_ss, halo_rs, fwd_ss, fwd_rs, own_sem, back_ss, back_rs, out_sem,
 ):
@@ -99,15 +99,7 @@
             pltpu.make_async_copy(
                 ens.at[m, levels], ensv.at[levels, inner, m, :], in_sem.at[part]).start()
 
-        def copy_kappa(m):
-            pltpu.make_async_copy(
-                kap.at[levels], ensv.at[levels, inner, MINE + m, :], in_sem.at[part]).start()
-
         loop(MINE, member)
-        loop(FIELDS - MINE, copy_kappa)
-
-    load_levels(0, 0, 1)
-    load_levels(1, 1, LEV - 1)
 
     barrier = pltpu.get_barrier_semaphore()
 
@@ -118,6 +110,12 @@
     loop(PEERS - 1, greet)
     for side in (east, west):
         pl.semaphore_signal(barrier, inc=1, device_id={"tile": side}, device_id_type=MESH)
+
+    load_kappa = pltpu.make_async_copy(kap, kapv, in_sem.at[2])
+    load_kappa.start()
+    load_levels(0, 0, 1)
+
+    load_levels(1, 1, LEV - 1)
 
     def clear(l):
         for y in (0, ROWS + 1):
@@ -129,34 +127,42 @@
     def wait_bytes(ref, sem):
         pltpu.make_async_copy(ref, ref, sem).wait()
 
-    wait_bytes(ensv.at[pl.ds(0, 1), inner], in_sem.at[0])
-
-    def step_one(l, b):
-        rows = [ensv[l, 8 * b + i, 0:MINE] for i in range(10)]
+    def spread_kappa(j):
+        l, b = j // 4, lax.rem(j, 4)
+        rows = kapv[l, pl.ds(pl.multiple_of(8 * b, 8), 8), :]
+        for i in range(8):
+            ensv[l, 8 * b + i + 1, MINE:FIELDS] = jnp.broadcast_to(rows[i:i + 1], (FIELDS - MINE, WIDE))
+
+    load_kappa.wait()
+    loop(4, spread_kappa)
+    wait_bytes(ensv.at[pl.ds(0, 1), inner, 0:MINE], in_sem.at[0])
+
+    def advanced(source, count, l, r):
+        rows = [source[l, 16 * r + i, 0:count] for i in range(18)]
         speed = adv[l]
-        for i in range(8):
+        result = []
+        for i in range(16):
             south, here, north = rows[i:i + 3]
-            kappa = ensv[l, 8 * b + i + 1, MINE:FIELDS]
+            kappa = ensv[l, 16 * r + i + 1, MINE:FIELDS]
             kappa = jnp.concatenate([kappa, kappa], axis=0)
-            u1[l, 8 * b + i + 1] = moved(here, turned(here, -1), turned(here, 1), north, south, kappa, speed)
-
-    def step_two(l, b):
-        rows = [u1[l, 8 * b + i] for i in range(10)]
-        speed = adv[l]
-        done = []
-        for i in range(8):
-            south, here, north = rows[i:i + 3]
-            kappa = ensv[l, 8 * b + i + 1, MINE:FIELDS]
-            kappa = jnp.concatenate([kappa, kappa], axis=0)
-            row = moved(here, turned(here, -1), turned(here, 1), north, south, kappa, speed)
-            done.append(turned(row, COLS * i))
-        r, h = b // 2, lax.rem(b, 2)
-        for c, patch in enumerate(sheared(done)):
-            snd[l, r * 8 + c, :, pl.ds(pl.multiple_of(h * WIDE, LANES), WIDE)] = patch
-
-    loop(4, lambda b: step_one(0, b))
-    loop(4, lambda b: step_two(0, b))
-    wait_bytes(ensv.at[pl.ds(1, LEV - 1), inner], in_sem.at[1])
+            result.append(moved(here, turned(here, -1), turned(here, 1), north, south, kappa, speed))
+        return result
+
+    def step_one(l, r):
+        for i, row in enumerate(advanced(ensv, MINE, l, r)):
+            u1[l, 16 * r + i + 1] = row
+
+    def step_two(l, r):
+        rows = advanced(u1, MINE, l, r)
+        for h in range(2):
+            done = [turned(rows[8 * h + i], COLS * i) for i in range(8)]
+            for c, patch in enumerate(sheared(done)):
+                snd[l, r * 8 + c, :, WIDE * h:WIDE * (h + 1)] = patch
+
+    loop(2, lambda r: step_one(0, r))
+    loop(2, lambda r: step_two(0, r))
+    loop(4 * LEV - 4, lambda j: spread_kappa(j + 4))
+    wait_bytes(ensv.at[pl.ds(1, LEV - 1), inner, 0:MINE], in_sem.at[1])
 
     lane = lax.broadcasted_iota(jnp.int32, (FIELDS, LANES), 1)
 
@@ -272,12 +278,12 @@
                     snd[l, r * 8 + c, :, WIDE * h + LANES * t:WIDE * h + LANES * (t + 1)] = tiles[t]
 
     def two_steps(l, follow):
-        def body(b):
-            step_two(l, b)
+        def body(r):
+            step_two(l, r)
             if follow:
-                step_one(l + 1, b)
-
-        loop(4, body)
+                step_one(l + 1, r)
+
+        loop(2, body)
 
     def finish_edges(l):
         mend_edges(l)
@@ -285,15 +291,14 @@
         send(l, True)
 
     send(0, False)
-    loop(4, lambda b: step_one(1, b))
+    loop(2, lambda r: step_one(1, r))
     two_steps(1, True)
+    send(1, False)
+    two_steps(2, True)
     to_west.wait()
     to_east.wait()
     finish_edges(0)
-    send(1, False)
     finish_edges(1)
-
-    two_steps(2, True)
     send(2, False)
     finish_edges(2)
     two_steps(3, False)
@@ -374,17 +379,16 @@
         backward_own(l).wait()
         wait_bytes(ret.at[l, pl.ds(0, K - MINE), :], back_rs.at[l])
 
-        def part(b):
-            r, h = b // 2, lax.rem(b, 2)
-            patches = [
-                ret[l, pl.ds(pl.multiple_of((r * 8 + c) * MINE, MINE), MINE),
-                    pl.ds(pl.multiple_of(h * WIDE, LANES), WIDE)]
-                for c in range(8)
-            ]
-            for i, row in enumerate(sheared(patches)):
-                field[l, 8 * b + i] = turned(row, -COLS * i)
-
-        loop(4, part)
+        def part(r):
+            for h in range(2):
+                patches = [
+                    ret[l, pl.ds(pl.multiple_of((r * 8 + c) * MINE, MINE), MINE), WIDE * h:WIDE * (h + 1)]
+                    for c in range(8)
+                ]
+                for i, row in enumerate(sheared(patches)):
+                    field[l, 16 * r + 8 * h + i] = turned(row, -COLS * i)
+
+        loop(2, part)
 
 
     loop(LEV, finish)
@@ -407,6 +411,7 @@
 def on_device(ensemble, kappa, advect, observed, counts):
     scratch = [
         pltpu.VMEM((LEV, PAD, FIELDS, WIDE), F32),
+        pltpu.VMEM((LEV, ROWS, WIDE), F32),
         *[pltpu.VMEM((LEV, FIELDS, LANES), F32)] * 2,
         *[pltpu.VMEM((LEV // 2, FIELDS, LANES), F32)] * 4,
         *[pltpu.VMEM((LEV, MINE, LANES), F32)] * 2,
@@ -419,7 +424,7 @@
         pltpu.VMEM((LEV, K, CELLS), F32),
         pltpu.VMEM((LEV, K, CELLS), F32),
         pltpu.VMEM((LEV, ROWS, MINE, WIDE), F32),
-        pltpu.SemaphoreType.DMA((2,)),
+        pltpu.SemaphoreType.DMA((3,)),
         *[pltpu.SemaphoreType.DMA((2,))] * 2,
         *[pltpu.SemaphoreType.DMA((LEV,))] * 2,
         pltpu.SemaphoreType.DMA((2 * LEV,)),

time: 84.7 us -> 83.3 us (0.983)
  Pallas kernels: 84.5 us -> 82.5 us
    pallas_call x1, Pallas kernels: 82.9 us -> 80.8 us  [on_device(): pl.pallas_call(kernel, out_shape=pltpu.VMEM((LEV, ROWS, MINE, WIDE), F32)...]
where the time goes in v4:
time: 83.3 us; the launch traced here: 82.5 us
  Pallas kernels  82.5 us (99%)
    pallas_call x1, Pallas kernels, on_device(): pl.pallas_call(kernel, out_shape=pltpu.VMEM((LEV, ROWS, MINE, WIDE), F32)...  80.8 us

profile of v4, /device:TPU:1, one launch (start us, length us, event | category | flops | bytes accessed | tf_op | source)
XLA Modules:
  0.0 82.5 jit_solution(13158449659816817980)
XLA Ops:
  0.0 80.8 %analysis.1.field = f32[4,32,16,384]{3,2,1,0:T(8,128)S(1)} custom-call(f32[16,4,32,384]{3,2,1,0:T(8,128)} %ens.1, f32[4,32,384]{2,1,0:T(8,128)} %kap.1, f32[4]{0:T(128)} %adv.1, f32[4,1,768]{2,1,0:T(1,128)} %bitcast.2, s32[4,1,768]{2,1,0:T(1,128)} %bitcast.3), custom_call_target="tpu_custom_call" | custom-call | tf_op jit(solution)/shard_map/analysis/pallas_call | solution.py:437
  80.8 1.7 %members_first.1 = f32[16,4,32,384]{3,2,1,0:T(8,128)} custom-call(f32[4,32,16,384]{3,2,1,0:T(8,128)S(1)} %analysis.1.field), custom_call_target="tpu_custom_call" | custom-call | tf_op jit(solution)/shard_map/members_first/pallas_call | solution.py:447

commit v5 on v4

--- a/solution.py
+++ b/solution.py
@@ -80,11 +80,21 @@
     return here + kappa * (east + west + north + south - 4.0 * here) + speed * (west - here)
 
 
+def unpack(patches_ref, rows_ref, r):
+    for h in range(2):
+        patches = [
+            patches_ref[pl.ds(pl.multiple_of((r * 8 + c) * MINE, MINE), MINE), WIDE * h:WIDE * (h + 1)]
+            for c in range(8)
+        ]
+        for i, row in enumerate(sheared(patches)):
+            rows_ref[16 * r + 8 * h + i] = turned(row, -COLS * i)
+
+
 def kernel(
-    ens, kap, adv, obs, cnt, field,
+    ens, kap, adv, obs, cnt, field, last,
     ensv, kapv, head, tail, send_w, send_e, recv_e, recv_w, mend_w, mend_e, u1,
-    snd, rcv, ph, pm, pl_, qh, ql, drive, inv, root, ana, ret, outv,
-    in_sem, halo_ss, halo_rs, fwd_ss, fwd_rs, own_sem, back_ss, back_rs, out_sem,
+    snd, rcv, ph, pm, pl_, qh, ql, drive, inv, root, ana, ret,
+    in_sem, halo_ss, halo_rs, fwd_ss, fwd_rs, own_sem, back_ss, back_rs,
 ):
     me = lax.axis_index("member")
     tile = lax.axis_index("tile")
@@ -166,18 +176,19 @@
 
     lane = lax.broadcasted_iota(jnp.int32, (FIELDS, LANES), 1)
 
-    def edges_of(l):
-        first = jnp.zeros((FIELDS, LANES), F32)
-        last = jnp.zeros((FIELDS, LANES), F32)
-        for y in range(ROWS):
-            ends = jnp.where(lane < 64, ensv[l, y + 1, :, 0:LANES], ensv[l, y + 1, :, 2 * LANES:3 * LANES])
-            ends = turned(ends, 4 * y)
-            first = jnp.where(lane // 4 == y, ends, first)
-            last = jnp.where(lane // 4 == (y - 1) % ROWS, ends, last)
-        head[l] = first
-        tail[l] = turned(last, 4)
-
-    loop(LEV, edges_of)
+    def edges_of(j):
+        for l in (2 * j, 2 * j + 1):
+            first = jnp.zeros((FIELDS, LANES), F32)
+            last = jnp.zeros((FIELDS, LANES), F32)
+            for y in range(ROWS):
+                ends = jnp.where(lane < 64, ensv[l, y + 1, :, 0:LANES], ensv[l, y + 1, :, 2 * LANES:3 * LANES])
+                ends = turned(ends, 4 * y)
+                first = jnp.where(lane // 4 == y, ends, first)
+                last = jnp.where(lane // 4 == (y - 1) % ROWS, ends, last)
+            head[l] = first
+            tail[l] = turned(last, 4)
+
+    loop(LEV // 2, edges_of)
     for j in range(LEV // 2):
         send_w[j] = jnp.where(lane % 4 < 2, head[2 * j], turned(head[2 * j + 1], 2))
         send_e[j] = jnp.where(lane % 4 < 2, turned(tail[2 * j + 1], -2), tail[2 * j])
@@ -198,15 +209,21 @@
     def forward_own(l):
         return pltpu.make_async_copy(snd.at[l, me], rcv.at[l, pl.ds(me * MINE, MINE), :], own_sem.at[l])
 
-    def backward(l, k):
-        peer = lax.rem(me + k + 1, PEERS)
-        return pltpu.make_async_remote_copy(
-            ana.at[l, pl.ds(peer * MINE, MINE), :], ret.at[l, pl.ds(me * MINE, MINE), :],
-            back_ss.at[l], back_rs.at[l], device_id={"member": peer}, device_id_type=MESH)
-
-    def backward_own(l):
-        at = pl.ds(me * MINE, MINE)
-        return pltpu.make_async_copy(ana.at[l, at, :], ret.at[l, at, :], own_sem.at[LEV + l])
+    def send_back(l, target):
+        mine = pl.ds(me * MINE, MINE)
+        pltpu.make_async_copy(ana.at[l, mine, :], target.at[mine, :], own_sem.at[LEV + l]).start()
+
+        def one(k):
+            peer = lax.rem(me + k + 1, PEERS)
+            pltpu.make_async_remote_copy(
+                ana.at[l, pl.ds(peer * MINE, MINE), :], target.at[mine, :], back_ss.at[l], back_rs.at[l],
+                device_id={"member": peer}, device_id_type=MESH).start()
+
+        loop(PEERS - 1, one)
+
+    def wait_back(l, target):
+        wait_bytes(target.at[pl.ds(0, MINE), :], own_sem.at[LEV + l])
+        wait_bytes(target.at[pl.ds(0, K - MINE), :], back_rs.at[l])
 
     def send(l, wanted):
         def one(k):
@@ -370,42 +387,37 @@
             cells = (ph[:, at], pm[:, at], pl_[:, at])
             ana[l, :, at] = mean[:, at] + product((w0, w1, w2), cells)
 
-        backward_own(l).start()
-        loop(PEERS - 1, lambda k: backward(l, k).start())
+        @pl.when(l < LEV - 1)
+        def _():
+            send_back(l, ret.at[l])
+
+        @pl.when(l == LEV - 1)
+        def _():
+            send_back(l, last)
 
     loop(LEV, analyse)
-
-    def finish(l):
-        backward_own(l).wait()
-        wait_bytes(ret.at[l, pl.ds(0, K - MINE), :], back_rs.at[l])
-
-        def part(r):
-            for h in range(2):
-                patches = [
-                    ret[l, pl.ds(pl.multiple_of((r * 8 + c) * MINE, MINE), MINE), WIDE * h:WIDE * (h + 1)]
-                    for c in range(8)
-                ]
-                for i, row in enumerate(sheared(patches)):
-                    field[l, 16 * r + 8 * h + i] = turned(row, -COLS * i)
-
-        loop(2, part)
-
-
-    loop(LEV, finish)
 
     def drain(l):
         wait_bytes(snd.at[l, pl.ds(0, PEERS - 1)], fwd_ss.at[l])
         wait_bytes(ana.at[l, pl.ds(0, K - MINE), :], back_ss.at[l])
 
-    loop(LEV, drain)
-
-
-def members_first(field, out, sem):
-    def copy(m):
-        return pltpu.make_async_copy(field.at[:, :, m, :], out.at[m], sem)
-
-    loop(MINE, lambda m: copy(m).start())
-    pltpu.make_async_copy(field, field, sem).wait()
+    def finish(l):
+        wait_back(l, ret.at[l])
+        loop(2, lambda r: unpack(ret.at[l], field.at[l], r))
+        drain(l)
+
+    loop(LEV - 1, finish)
+    drain(LEV - 1)
+    wait_back(LEV - 1, last)
+
+
+def members_first(field, last, out, spare, sems):
+    early = pl.ds(0, LEV - 1)
+    loop(MINE, lambda m: pltpu.make_async_copy(field.at[:, :, m, :], out.at[m, early], sems.at[0]).start())
+    loop(2, lambda r: unpack(last, spare, r))
+    loop(MINE, lambda m: pltpu.make_async_copy(spare.at[:, m, :], out.at[m, LEV - 1], sems.at[1]).start())
+    pltpu.make_async_copy(field, field, sems.at[0]).wait()
+    pltpu.make_async_copy(spare, spare, sems.at[1]).wait()
 
 
 def on_device(ensemble, kappa, advect, observed, counts):
@@ -422,23 +434,21 @@
         pltpu.VMEM((K, 1), F32),
         *[pltpu.VMEM((K, K), F32)] * 2,
         pltpu.VMEM((LEV, K, CELLS), F32),
-        pltpu.VMEM((LEV, K, CELLS), F32),
-        pltpu.VMEM((LEV, ROWS, MINE, WIDE), F32),
+        pltpu.VMEM((LEV - 1, K, CELLS), F32),
         pltpu.SemaphoreType.DMA((3,)),
         *[pltpu.SemaphoreType.DMA((2,))] * 2,
         *[pltpu.SemaphoreType.DMA((LEV,))] * 2,
         pltpu.SemaphoreType.DMA((2 * LEV,)),
         *[pltpu.SemaphoreType.DMA((LEV,))] * 2,
-        pltpu.SemaphoreType.DMA((LEV,)),
     ]
     vmem = pl.BlockSpec(memory_space=pltpu.VMEM)
     whole = pl.BlockSpec(memory_space=pl.ANY)
     smem = pl.BlockSpec(memory_space=pltpu.SMEM)
-    members_last = pl.pallas_call(
+    most, last = pl.pallas_call(
         kernel,
-        out_shape=pltpu.VMEM((LEV, ROWS, MINE, WIDE), F32),
+        out_shape=(pltpu.VMEM((LEV - 1, ROWS, MINE, WIDE), F32), pltpu.VMEM((K, CELLS), F32)),
         in_specs=[whole, whole, smem, vmem, vmem],
-        out_specs=vmem,
+        out_specs=(vmem, vmem),
         scratch_shapes=scratch,
         compiler_params=pltpu.CompilerParams(
             collective_id=0, has_side_effects=True, vmem_limit_bytes=56 * 1024 * 1024),
@@ -447,12 +457,12 @@
     return pl.pallas_call(
         members_first,
         out_shape=jax.ShapeDtypeStruct((MINE, LEV, ROWS, WIDE), F32),
-        in_specs=[whole],
+        in_specs=[whole, vmem],
         out_specs=whole,
-        scratch_shapes=[pltpu.SemaphoreType.DMA],
-        compiler_params=pltpu.CompilerParams(vmem_limit_bytes=1024 * 1024),
+        scratch_shapes=[pltpu.VMEM((ROWS, MINE, WIDE), F32), pltpu.SemaphoreType.DMA((2,))],
+        compiler_params=pltpu.CompilerParams(vmem_limit_bytes=4 * 1024 * 1024),
         name="members_first",
-    )(members_last)
+    )(most, last)
 
 
 def solution(mesh):

time: 83.3 us -> 82.6 us (level)
  no operation moved by 1% of the time
where the time goes in v5:
time: 82.6 us; the launch traced here: 82.3 us
  Pallas kernels  82.3 us (100%)
    pallas_call x1, Pallas kernels, on_device(): pl.pallas_call(kernel, out_shape=(pltpu.VMEM((LEV - 1, ROWS, MINE, WIDE),...  80.7 us
    pallas_call x1, Pallas kernels, on_device(): pl.pallas_call(members_first, out_shape=jax.ShapeDtypeStruct((MINE, LEV,...  1.66 us

profile of v5, /device:TPU:1, one launch (start us, length us, event | category | flops | bytes accessed | tf_op | source)
XLA Modules:
  0.0 82.3 jit_solution(11134794356791775144)
XLA Ops:
  0.0 80.7 %analysis.1 = (f32[3,32,16,384]{3,2,1,0:T(8,128)S(1)}, f32[256,768]{1,0:T(8,128)S(1)}) custom-call(f32[16,4,32,384]{3,2,1,0:T(8,128)} %ens.1, f32[4,32,384]{2,1,0:T(8,128)} %kap.1, f32[4]{0:T(128)} %adv.1, f32[4,1,768]{2,1,0:T(1,128)} %bitcast.2, s32[4,1,768]{2,1,0:T(1,128)} %bitcast.3), custom_call_target="tpu_custom_call" | custom-call | tf_op jit(solution)/shard_map/analysis/pallas_call | solution.py:447
  80.7 1.7 %members_first.1 = f32[16,4,32,384]{3,2,1,0:T(8,128)} custom-call(f32[3,32,16,384]{3,2,1,0:T(8,128)S(1)} %get-tuple-element.7.field, f32[256,768]{1,0:T(8,128)S(1)} %get-tuple-element.8.last), custom_call_target="tpu_custom_call" | custom-call | tf_op jit(solution)/shard_map/members_first/pallas_call | solution.py:457

commit v6 on v5

--- a/solution.py
+++ b/solution.py
@@ -371,13 +371,13 @@
         def newton(i):
             held, base = split3(inv[...]), split3(root[...])
             factor = split3(1.5 * eye - 0.5 * product(held, base))
-            inv[...] = product(held, factor)
+            inv[...] = product(factor, held)
             root[...] = product(base, factor)
 
         loop(ITERS - 2, newton)
         held, base = split3(inv[...]), split3(root[...])
         factor = split3(1.5 * eye - 0.5 * product(held, base))
-        half = product(held, factor) * lax.rsqrt(scale)
+        half = product(factor, held) * lax.rsqrt(scale)
 
         once = jnp.sum(half * drive[...], axis=0, keepdims=True)
         twice = jnp.sum(half * once, axis=1, keepdims=True)

time: 82.6 us -> 83.2 us (level); the launches traced: 82.3 us -> 81.6 us
  no operation moved by 1% of the time
where the time goes in v6:
time: 83.2 us; the launch traced here: 81.6 us
  Pallas kernels  81.6 us (98%)
    pallas_call x1, Pallas kernels, on_device(): pl.pallas_call(kernel, out_shape=(pltpu.VMEM((LEV - 1, ROWS, MINE, WIDE),...  79.9 us

profile of v6, /device:TPU:1, one launch (start us, length us, event | category | flops | bytes accessed | tf_op | source)
XLA Modules:
  0.0 81.6 jit_solution(18321319037407144318)
XLA Ops:
  0.0 79.9 %analysis.1 = (f32[3,32,16,384]{3,2,1,0:T(8,128)S(1)}, f32[256,768]{1,0:T(8,128)S(1)}) custom-call(f32[16,4,32,384]{3,2,1,0:T(8,128)} %ens.1, f32[4,32,384]{2,1,0:T(8,128)} %kap.1, f32[4]{0:T(128)} %adv.1, f32[4,1,768]{2,1,0:T(1,128)} %bitcast.2, s32[4,1,768]{2,1,0:T(1,128)} %bitcast.3), custom_call_target="tpu_custom_call" | custom-call | tf_op jit(solution)/shard_map/analysis/pallas_call | solution.py:447
  79.9 1.7 %members_first.1 = f32[16,4,32,384]{3,2,1,0:T(8,128)} custom-call(f32[3,32,16,384]{3,2,1,0:T(8,128)S(1)} %get-tuple-element.7.field, f32[256,768]{1,0:T(8,128)S(1)} %get-tuple-element.8.last), custom_call_target="tpu_custom_call" | custom-call | tf_op jit(solution)/shard_map/members_first/pallas_call | solution.py:457
